TPU v7x, 512 devices: a whole 4x8x8 slice. The times are simulated.
512 devices in a mesh: freq: 128 (over y, z, core), rows: 4 (over x).
Axes of the slice: x: 4, y: 8, z: 8, core: 2. Of those that a mesh axis runs over, the one named last changes fastest.
Arguments:
- direct: float32 [96, 1536, 256], P('rows', 'freq'), may hold values from -6 to 6
- current: float32 [96, 1536, 256], P('rows', 'freq'), may hold values from -6 to 6
- onsets: int32 [96, 1536], P('rows', 'freq'), may hold values from 32 to 128
- reflection: bfloat16 [2, 128, 1536, 1536], P(None, 'freq', None, 'rows'), may hold values from -0.15625 to 0.15625
Outputs:
- upgoing: float32 [96, 1536, 256], P('rows', 'freq')
- downgoing: float32 [96, 1536, 256], P('rows', 'freq')
All inputs are finite; a program needn't handle non-finite values.
Results may differ from a plain program's by a relative error of at most 0.0031.
Values may be sent and summed in bfloat16 or wider, within the bound.
A program may use at most 64 MiB of HBM per device.

v0:
```python
import math

import jax
import jax.numpy as jnp
from jax import lax
from jax.sharding import PartitionSpec as P


def tables(nfreq, ntime):
    freqs = jnp.arange(nfreq)[:, None]
    times = jnp.arange(ntime)[None, :]
    phase = (freqs * times % ntime).astype(jnp.float32) * jnp.float32(2.0 * math.pi / ntime)
    cosine = jnp.cos(phase)
    sine = jnp.sin(phase)
    weights = jnp.where(freqs == 0, 1.0, 2.0).astype(jnp.float32) / jnp.float32(ntime)
    forward = jnp.stack([cosine, -sine])
    inverse = jnp.stack([weights * cosine, -weights * sine])
    return (forward, inverse)


def to_freq(field, forward):
    spectrum = jnp.einsum("ckt,prt->ckpr", forward, field, precision=lax.Precision.HIGHEST).astype(
        jnp.bfloat16
    )
    return lax.all_to_all(spectrum, "freq", split_axis=1, concat_axis=3, tiled=True)


def to_time(spectrum, inverse):
    gathered = lax.all_to_all(spectrum, "freq", split_axis=3, concat_axis=1, tiled=True)
    return jnp.einsum("ckt,ckpr->prt", inverse, gathered, precision=lax.Precision.HIGHEST)


def back_product(spectra, columns):
    real_p = jnp.einsum(
        "wpa,wab->wpb", spectra[0], columns[0], preferred_element_type=jnp.float32
    ) + jnp.einsum("wpa,wab->wpb", spectra[1], columns[1], preferred_element_type=jnp.float32)
    imag_p = jnp.einsum(
        "wpa,wab->wpb", spectra[1], columns[0], preferred_element_type=jnp.float32
    ) - jnp.einsum("wpa,wab->wpb", spectra[0], columns[1], preferred_element_type=jnp.float32)
    return jnp.stack([real_p, imag_p])


def shards(direct, current, onsets, reflection):
    ntime = current.shape[2]
    forward, inverse = tables(ntime // 2, ntime)
    samples = jnp.arange(ntime)
    starts = onsets[:, :, None]
    window = ((samples < starts) | (samples > ntime - starts)).astype(jnp.float32)
    spec_down = to_freq(current, forward)
    by_columns = lax.all_to_all(spec_down, "rows", split_axis=3, concat_axis=2, tiled=True)
    real_p = jnp.einsum(
        "wpb,wab->wpa", by_columns[0], reflection[0], preferred_element_type=jnp.float32
    ) - jnp.einsum("wpb,wab->wpa", by_columns[1], reflection[1], preferred_element_type=jnp.float32)
    imag_p = jnp.einsum(
        "wpb,wab->wpa", by_columns[0], reflection[1], preferred_element_type=jnp.float32
    ) + jnp.einsum("wpb,wab->wpa", by_columns[1], reflection[0], preferred_element_type=jnp.float32)
    partial_value = jnp.stack([real_p, imag_p])
    block = lax.psum_scatter(partial_value, "rows", scatter_dimension=3, tiled=True)
    summed = lax.all_to_all(block, "rows", split_axis=2, concat_axis=3, tiled=True)
    upgoing = to_time(summed, inverse) * window
    spec_up = to_freq(upgoing, forward)
    product = back_product(lax.all_gather(spec_up, "rows", axis=2, tiled=True), reflection)
    mine = lax.all_to_all(product, "rows", split_axis=2, concat_axis=3, tiled=True)
    downgoing = direct + to_time(mine, inverse) * window
    return (upgoing, downgoing)


def solution(mesh):
    in_specs = (
        P("rows", "freq", None),
        P("rows", "freq", None),
        P("rows", "freq"),
        P(None, "freq", None, "rows"),
    )
    out_specs = (P("rows", "freq", None), P("rows", "freq", None))
    return jax.shard_map(shards, mesh=mesh, in_specs=in_specs, out_specs=out_specs, check_vma=False)
```

profile of v0, /device:TPU:1, one launch (start us, length us, event | category | flops | bytes accessed | tf_op | source)
XLA Modules:
  0.0 232.9 jit_solution(1184760187070387659)
XLA Ops:
  10.7 31.6 %all_to_all.123 = bf16[128,2,288]{2,1,0:T(2,128)(2,1)S(1)} all-to-all(bf16[128,2,288]{2,1,0:T(2,128)(2,1)S(1)} %reshape.224), channel_id=1, replica_groups=mesh['freq'=128,'rows'=4] {'freq'}, dimensions={0} | all-to-all | bytes 294912 | tf_op jit(solution)/shard_map/all_to_all | solution.py:25
  43.2 1.7 reshape.226
  44.8 9.0 %all_to_all.124 = bf16[4,2,9216]{2,1,0:T(2,128)(2,1)} all-to-all(bf16[4,2,9216]{2,1,0:T(2,128)(2,1)} %reshape.226), channel_id=1, replica_groups=mesh['freq'=128,'rows'=4] {'rows'}, dimensions={0} | all-to-all | bytes 294912 | tf_op jit(solution)/shard_map/all_to_all | solution.py:50
  53.9 2.0 reshape.227
  55.8 1.6 copy.81
  61.6 20.6 %reduce-scatter.2.cloned.1.call-done = f32[2,1,96,384]{3,2,1,0:T(8,128)} async-done(((f32[2,1,96,1536]{3,2,1,0:T(8,128)}), f32[2,1,96,384]{3,2,1,0:T(8,128)}) %reduce-scatter.2.cloned.1.call-update) | async-done | bytes 294928 | tf_op jit(solution)/shard_map/reduce_scatter | solution.py:58
  83.4 8.1 %all_to_all.125 = f32[2,1,96,384]{3,1,0,2:T(1,128)S(1)} all-to-all(f32[2,1,96,384]{3,1,0,2:T(1,128)S(1)} %copy.66), channel_id=1, replica_groups=mesh['freq'=128,'rows'=4] {'rows'}, dimensions={2} | all-to-all | bytes 589824 | tf_op jit(solution)/shard_map/all_to_all | solution.py:59
  91.8 2.1 copy.82
  93.8 4.4 %reshape.228 = f32[128,1,576]{2,1,0:T(1,128)} reshape(f32[1536,1,2,24]{3,2,1,0:T(2,128)} %bitcast.122) | data formatting | bytes 589824
  98.3 17.0 %all-to-all-start.3 = ((f32[128,1,576]{2,1,0:T(1,128)}), f32[128,1,576]{2,1,0:T(1,128)S(1)}, u32[]{:S(2)}, u32[]{:S(2)}) async-start(f32[128,1,576]{2,1,0:T(1,128)} %reshape.228), calls=%async_computation.4 | async-start | bytes 655360 | tf_op jit(solution)/shard_map/all_to_all | solution.py:29
  116.5 14.3 %all-to-all-done.3 = f32[128,1,576]{2,1,0:T(1,128)S(1)} async-done(((f32[128,1,576]{2,1,0:T(1,128)}), f32[128,1,576]{2,1,0:T(1,128)S(1)}, u32[]{:S(2)}, u32[]{:S(2)}) %all-to-all-start.3) | async-done | bytes 294944 | tf_op jit(solution)/shard_map/all_to_all | solution.py:29
  132.9 3.4 %reshape.229 = f32[1536,1,2,24]{3,2,1,0:T(2,128)} reshape(f32[128,576]{1,0:T(8,128)S(1)} %reduce) | data formatting | bytes 589824
  136.2 2.5 %copy.69 = f32[2,1,24,128,12]{3,2,0,4,1:T(8,128)S(1)} copy(f32[2,1,24,128,12]{2,0,4,3,1:T(2,128)} %bitcast.123) | data formatting | bytes 589824 | tf_op jit(solution)/shard_map/all_to_all | solution.py:29
  141.0 2.0 copy.70
  143.0 1.7 reshape.230
  144.8 21.5 %all_to_all.126 = bf16[128,2,288]{2,1,0:T(2,128)(2,1)} all-to-all(bf16[128,2,288]{2,1,0:T(2,128)(2,1)} %reshape.230), channel_id=1, replica_groups=mesh['freq'=128,'rows'=4] {'freq'}, dimensions={0} | all-to-all | bytes 294912 | tf_op jit(solution)/shard_map/all_to_all | solution.py:25
  166.3 1.8 reshape.231
  168.1 1.6 copy.71
  169.7 10.8 %all_gather.3 = bf16[2,1,96,1536]{3,0,1,2:T(2,128)(2,1)S(1)} all-gather(bf16[2,1,24,1536]{3,0,1,2:T(2,128)(2,1)} %copy.71), channel_id=1, replica_groups=mesh['freq'=128,'rows'=4] {'rows'}, dimensions={2}, use_global_device_ids=true | all-gather | bytes 737280 | tf_op jit(solution)/shard_map/all_gather | solution.py:62
  183.1 8.8 %all_to_all.127 = f32[2,1,96,384]{3,1,0,2:T(1,128)S(1)} all-to-all(f32[2,1,96,384]{3,1,0,2:T(1,128)S(1)} %copy.74), channel_id=1, replica_groups=mesh['freq'=128,'rows'=4] {'rows'}, dimensions={2} | all-to-all | bytes 589824 | tf_op jit(solution)/shard_map/all_to_all | solution.py:63
  193.0 2.3 reshape.232
  195.3 25.2 %all_to_all.128 = f32[128,1,576]{2,1,0:T(1,128)S(1)} all-to-all(f32[128,1,576]{2,1,0:T(1,128)S(1)} %reshape.232), channel_id=1, replica_groups=mesh['freq'=128,'rows'=4] {'freq'}, dimensions={0} | all-to-all | bytes 589824 | tf_op jit(solution)/shard_map/all_to_all | solution.py:29
  220.6 1.5 reduce.1
  222.1 2.2 reshape.233
  (64 shorter events, 20.9 us)
Async XLA Ops:
  7.2 1.3 copy-start
  7.2 75.0 %reduce-scatter.2.cloned.1.call-start = ((), (), s32[]{:S(2)}) async-start(), calls=%async_computation.8 | async-start | bytes 1474560 | tf_op jit(solution)/shard_map/reduce_scatter | solution.py:58
  7.8 0.7 copy-start.7
  7.8 0.7 copy-start.9
  43.1 15.3 %copy-start.1 = (bf16[2,1,1536,384]{3,2,1,0:T(8,128)(2,1)S(1)}, bf16[2,1,1536,384]{3,2,1,0:T(8,128)(2,1)}, u32[]{:S(2)}) copy-start(bf16[2,1,1536,384]{3,2,1,0:T(8,128)(2,1)} %param.7) | copy-start | bytes 7077892
  93.8 21.4 %copy-start.12 = (s32[24,12]{0,1:T(8,128)S(1)}, s32[24,12]{0,1:T(8,128)}, u32[]{:S(2)}) copy-start(s32[24,12]{0,1:T(8,128)} %param.6) | copy-start | bytes 3460
  98.3 32.5 %all-to-all-start.3 = ((f32[128,1,576]{2,1,0:T(1,128)}), f32[128,1,576]{2,1,0:T(1,128)S(1)}, u32[]{:S(2)}, u32[]{:S(2)}) async-start(f32[128,1,576]{2,1,0:T(1,128)} %reshape.228), calls=%async_computation.4 | async-start | bytes 655360 | tf_op jit(solution)/shard_map/all_to_all | solution.py:29
  116.5 22.3 %copy-start.2 = (f32[1,128,256]{2,1,0:T(8,128)}, f32[1,128,256]{2,1,0:T(8,128)S(1)}, u32[]{:S(2)}) copy-start(f32[1,128,256]{2,1,0:T(8,128)S(1)} %get-tuple-element.8) | copy-start | bytes 393220
  136.2 2.5 %copy-start.4 = (f32[1,128,256]{2,1,0:T(8,128)S(1)}, f32[1,128,256]{2,1,0:T(8,128)}, u32[]{:S(2)}) copy-start(f32[1,128,256]{2,1,0:T(8,128)} %get-tuple-element.9) | copy-start | bytes 393220
  136.2 3.7 %copy-start.8 = (f32[1,128,256]{2,1,0:T(8,128)S(1)}, f32[1,128,256]{2,1,0:T(8,128)}, u32[]{:S(2)}) copy-start(f32[1,128,256]{2,1,0:T(8,128)} %copy-done.7) | copy-start | bytes 393220
  136.2 3.7 %copy-start.10 = (f32[1,128,256]{2,1,0:T(8,128)S(1)}, f32[1,128,256]{2,1,0:T(8,128)}, u32[]{:S(2)}) copy-start(f32[1,128,256]{2,1,0:T(8,128)} %copy-done.9) | copy-start | bytes 393220
  139.2 0.7 copy-start.6
  222.0 2.9 %copy-start.3 = (f32[1,128,256]{2,1,0:T(8,128)S(1)}, f32[1,128,256]{2,1,0:T(8,128)}, u32[]{:S(2)}) copy-start(f32[1,128,256]{2,1,0:T(8,128)} %copy-done.2) | copy-start | bytes 393220
  222.0 2.9 %copy-start.5 = (f32[1,128,256]{2,1,0:T(8,128)S(1)}, f32[1,128,256]{2,1,0:T(8,128)}, u32[]{:S(2)}) copy-start(f32[1,128,256]{2,1,0:T(8,128)} %get-tuple-element.9) | copy-start | bytes 393220
  222.1 2.9 %copy-start.11 = (f32[24,12,256]{2,0,1:T(8,128)S(1)}, f32[24,12,256]{2,0,1:T(8,128)}, u32[]{:S(2)}) copy-start(f32[24,12,256]{2,0,1:T(8,128)} %param.4) | copy-start | bytes 884740
Sparse Core Ops, SparseCore 0:
  61.7 20.4 reduce-scatter.1
where the time goes:
time: 234 us; the launch traced here: 233 us
  blocking collectives  115 us (49%)
  local copies, waits for them, and re-layouts  39.3 us (17%)
  waiting for transfers between devices  34.9 us (15%)
  starting transfers between devices  17 us (7%)
  between operations  14.4 us (6%)
  matrix products  6.48 us (3%)
  other arithmetic  5.79 us (2%)
    all_to_all x2, blocking collectives, to_freq(): lax.all_to_all(spectrum, 'freq', split_axis=1, concat_axis=3, tiled=True)  53.1 us
    all_to_all x1, blocking collectives, to_time(): lax.all_to_all(spectrum, 'freq', split_axis=3, concat_axis=1, tiled=True)  25.2 us
    unnamed x38, local copies, waits for them, and re-layouts  23.1 us
    reduce_scatter x1, waiting for transfers between devices, shards(): lax.psum_scatter(partial_value, 'rows', scatter_dimension=3, tiled=True)  20.6 us
    all_to_all x1, starting transfers between devices, to_time(): lax.all_to_all(spectrum, 'freq', split_axis=3, concat_axis=1, tiled=True)  17 us
    all_to_all x1, waiting for transfers between devices, to_time(): lax.all_to_all(spectrum, 'freq', split_axis=3, concat_axis=1, tiled=True)  14.3 us
    all_gather x1, blocking collectives, shards(): lax.all_gather(spec_up, 'rows', axis=2, tiled=True)  10.8 us
    all_to_all x1, blocking collectives, shards(): lax.all_to_all(spec_down, 'rows', split_axis=3, concat_axis=2, tiled=True)  9.03 us
  transfers between devices with their start and end apart: 2, of which 2 were waited for; matrix products, arithmetic and copies ran while one was open for 1% of the time, Pallas kernels for 0%

commit v1 on v0

v1 whole, which is shorter than its diff:
```python
import functools
import math

import jax
import jax.numpy as jnp
import ml_dtypes
import numpy as np
from jax import lax
from jax.experimental import pallas as pl
from jax.experimental.pallas import tpu as pltpu
from jax.sharding import PartitionSpec as P

MESH = pl.DeviceIdType.MESH
PAD = 32
TILE = 128
PEAK = 32000.0
SPOT = 31
F32, BF16, I16 = jnp.float32, jnp.bfloat16, jnp.int16


def split(table):
    high = table.astype(ml_dtypes.bfloat16)
    low = (table - high.astype(np.float64)).astype(ml_dtypes.bfloat16)
    return np.stack([high, low])


def tables(nfreq, ntime):
    phase = (np.arange(nfreq)[:, None] * np.arange(ntime)[None, :] % ntime) * (2.0 * math.pi / ntime)
    weights = np.where(np.arange(nfreq) == 0, 1.0, 2.0)[:, None] / ntime
    forward = np.stack([np.cos(phase), -np.sin(phase)], axis=1)
    inverse = forward * weights[:, None]
    return (
        split(forward.reshape(2 * nfreq, ntime)),
        split(inverse.reshape(2 * nfreq, ntime)),
    )


def halves(value):
    high = value.astype(BF16)
    return high, (value - high.astype(F32)).astype(BF16)


def dot(a, b, contract):
    return lax.dot_general(a, b, (contract, ((), ())), preferred_element_type=F32)


def swap_blocks(arrays):
    shape = arrays[0].shape
    block = lax.broadcasted_iota(jnp.int32, shape, len(shape) - 1) // PAD
    low, even = block < 2, block % 2 == 0
    a0, a1, a2, a3 = arrays
    turn = lambda a, shift: pltpu.roll(a, shift, len(shape) - 1)
    b0, b2 = jnp.where(low, a0, turn(a2, 64)), jnp.where(low, turn(a0, 64), a2)
    b1, b3 = jnp.where(low, a1, turn(a3, 64)), jnp.where(low, turn(a1, 64), a3)
    c0, c1 = jnp.where(even, b0, turn(b1, 32)), jnp.where(even, turn(b0, 96), b1)
    c2, c3 = jnp.where(even, b2, turn(b3, 32)), jnp.where(even, turn(b2, 96), b3)
    return [c0, c1, c2, c3]


def encode(value):
    lane = lax.broadcasted_iota(jnp.int32, value.shape, 1)
    largest = jnp.max(jnp.abs(value), axis=1, keepdims=True)
    power = jnp.ceil(jnp.log2(jnp.maximum(largest, 1e-30)) + 1e-3)
    codes = jnp.round(value * (jnp.exp2(-power) * PEAK))
    return jnp.where(lane == SPOT, power, codes).astype(jnp.int32).astype(I16)


def decode(codes):
    codes = codes.astype(jnp.int32).astype(F32)
    return codes * (jnp.exp2(codes[:, SPOT : SPOT + 1]) * (1.0 / PEAK))


def kernel(
    dims,
    direct_hbm, current_hbm, onsets_ref, reflection_hbm, forward_hbm, inverse_hbm,
    up_ref, down_ref,
    direct_ref, current_ref, refl, back, forward_ref, inverse_ref, field,
    send_a, got_a, cols_a, stage, weights,
    partial, blocks, send_s, got_s, send_b, got_b,
    send_c, got_c, all_c, full, product,
    send_e, got_e, got_d,
    load_sem, send_sem, recv_sem,
):
    nf, nx, nr, npt = dims
    nb = nf // nx
    rows = 2 * nf
    wide = nr * PAD
    f, x = lax.axis_index("freq"), lax.axis_index("rows")

    loads = [
        pltpu.make_async_copy(source, target, load_sem.at[i])
        for i, (source, target) in enumerate(
            [
                (current_hbm, current_ref),
                (forward_hbm, forward_ref),
                (reflection_hbm, refl),
                (inverse_hbm, inverse_ref),
                (direct_hbm, direct_ref),
            ]
        )
    ]
    for load in loads:
        load.start()

    barrier = pltpu.get_barrier_semaphore()

    def greet(step, carry):
        pl.semaphore_signal(barrier, inc=1, device_id=(lax.rem(f + step, nf), x), device_id_type=MESH)
        return carry

    lax.fori_loop(1, nf, greet, 0)
    for step in range(1, nx):
        pl.semaphore_signal(barrier, inc=1, device_id=(f, lax.rem(x + step, nx)), device_id_type=MESH)

    def exchange(source, target, which):
        def one(step, carry):
            peer = lax.rem(f + step, nf)
            pltpu.make_async_remote_copy(
                src_ref=source.at[peer], dst_ref=target.at[f],
                send_sem=send_sem.at[which], recv_sem=recv_sem.at[which],
                device_id=(peer, x), device_id_type=MESH,
            ).start()
            return carry

        lax.fori_loop(1, nf, one, 0, unroll=min(8, nf - 1))
        target[f] = source[f]

    def finish(source, target, which, count):
        pltpu.make_async_copy(source.at[pl.ds(0, count)], source.at[pl.ds(0, count)], send_sem.at[which]).wait()
        pltpu.make_async_copy(target.at[pl.ds(0, count)], target.at[pl.ds(0, count)], recv_sem.at[which]).wait()

    def to_rows(pick, target, which):
        for step in range(1, nx):
            peer = lax.rem(x + step, nx)
            pltpu.make_async_remote_copy(
                src_ref=pick(peer), dst_ref=target.at[x],
                send_sem=send_sem.at[which], recv_sem=recv_sem.at[which],
                device_id=(f, peer), device_id_type=MESH,
            ).start()

    def transform():
        high, low = halves(field[...])
        spectra = (
            dot(forward_ref[0], high, ((1,), (1,)))
            + dot(forward_ref[0], low, ((1,), (1,)))
            + dot(forward_ref[1], high, ((1,), (1,)))
        )
        return spectra.astype(BF16).reshape(nf, 2, wide)

    def invert(messages):
        high, low = halves(decode(messages.reshape(rows, wide)))
        return (
            dot(high, inverse_ref[0], ((0,), (0,)))
            + dot(low, inverse_ref[0], ((0,), (0,)))
            + dot(high, inverse_ref[1], ((0,), (0,)))
        )

    samples = lax.broadcasted_iota(jnp.int32, (npt, 2 * nf), 1)

    def window(r):
        start = onsets_ref[:, r : r + 1]
        return (samples < start) | (samples > 2 * nf - start)

    field[...] = jnp.zeros_like(field)
    loads[0].wait()
    for r in range(nr):
        field[r * PAD : r * PAD + npt, :] = current_ref[:, r, :]
    loads[1].wait()
    send_a[...] = transform()
    pl.semaphore_wait(barrier, nf - 1 + nx - 1)
    exchange(send_a, got_a, 0)
    loads[2].wait()
    for c in range(2):
        back[c] = jnp.swapaxes(refl[c], 0, 1)
    finish(send_a, got_a, 0, nf - 1)

    to_rows(lambda peer: got_a.at[pl.ds(peer * nb, nb)], cols_a, 1)
    cols_a[x] = got_a[pl.ds(x * nb, nb)]
    finish(cols_a, cols_a, 1, nx - 1)

    def spread(messages, count, target):
        for i in range(nx):
            message = messages(i).reshape(2 * count, wide).astype(F32)
            for t in range(nr // 4):
                stage[i, t, : 2 * count] = message[:, t * TILE : (t + 1) * TILE]
        for t in range(nr // 4):
            for c in range(2):
                parts = swap_blocks(
                    [stage[i, t, pl.ds(c, count, stride=2), :] for i in range(nx)]
                )
                for j in range(4):
                    target[c, pl.ds(4 * t + j, count, stride=nr), :] = parts[j]

    def gather(source, count, target):
        for t in range(nr // 4):
            for c in range(2):
                parts = swap_blocks(
                    [source[c, pl.ds(4 * t + j, count, stride=nr), :] for j in range(4)]
                )
                for i in range(nx):
                    target[i, t, pl.ds(c, count, stride=2), :] = parts[i]

    def joined(source, i, count):
        return jnp.concatenate([source[i, t, :count] for t in range(nr // 4)], axis=1)

    spread(lambda i: cols_a[i], nb, weights)
    real, imag = weights[0].astype(BF16), weights[1].astype(BF16)
    sums = dot(refl[0], jnp.concatenate([real, imag], axis=1), ((1,), (0,))) + dot(
        refl[1], jnp.concatenate([-imag, real], axis=1), ((1,), (0,))
    )
    partial[0], partial[1] = sums[:, :TILE], sums[:, TILE:]
    gather(partial, nf, blocks)
    for i in range(nx):
        send_s[i] = encode(joined(blocks, i, rows))
    to_rows(lambda peer: send_s.at[peer], got_s, 2)
    finish(send_s, got_s, 2, nx - 1)
    total = joined(blocks, x, rows)
    for step in range(1, nx):
        total = total + decode(got_s[lax.rem(x + step, nx)])

    send_b[...] = encode(total).reshape(nf, 2, wide)
    exchange(send_b, got_b, 3)
    loads[3].wait()
    finish(send_b, got_b, 3, nf - 1)
    signal = invert(got_b[...])
    for r in range(nr):
        kept = jnp.where(window(r), signal[r * PAD : r * PAD + npt], 0.0)
        up_ref[:, r, :] = kept
        field[r * PAD : r * PAD + npt, :] = kept

    send_c[...] = transform()
    exchange(send_c, got_c, 4)
    finish(send_c, got_c, 4, nf - 1)
    to_rows(lambda peer: got_c, all_c, 5)
    all_c[x] = got_c[...]
    finish(all_c, all_c, 5, nx - 1)

    spread(lambda i: all_c[i], nf, full)
    real, imag = full[0].astype(BF16), full[1].astype(BF16)
    sums = dot(back[0], jnp.concatenate([real, imag], axis=1), ((1,), (0,))) + dot(
        back[1], jnp.concatenate([imag, -real], axis=1), ((1,), (0,))
    )
    product[0], product[1] = sums[:, :TILE], sums[:, TILE:]
    gather(product, nb, stage)
    for i in range(nx):
        send_e[i] = encode(joined(stage, i, 2 * nb)).reshape(nb, 2, wide)
    to_rows(lambda peer: send_e.at[peer], got_e, 6)
    got_e[x] = send_e[x]
    finish(send_e, got_e, 6, nx - 1)

    def last(step, carry):
        peer = lax.rem(f + step, nf)
        pltpu.make_async_remote_copy(
            src_ref=got_e.at[peer // nb, lax.rem(peer, nb)], dst_ref=got_d.at[f],
            send_sem=send_sem.at[7], recv_sem=recv_sem.at[7],
            device_id=(peer, x), device_id_type=MESH,
        ).start()
        return carry

    lax.fori_loop(1, nf, last, 0, unroll=min(8, nf - 1))
    got_d[f] = got_e[f // nb, lax.rem(f, nb)]
    loads[4].wait()
    finish(send_c, got_d, 7, nf - 1)
    signal = invert(got_d[...])
    for r in range(nr):
        kept = jnp.where(window(r), signal[r * PAD : r * PAD + npt], 0.0)
        down_ref[:, r, :] = direct_ref[:, r, :] + kept


def shards(nf, nx, direct, current, onsets, reflection):
    npt, nr, ntime = current.shape
    nb, wide = nf // nx, nr * PAD
    sources, columns = nf * nr, nb * nr
    forward, inverse = tables(nf, ntime)
    reflection = reflection.reshape(2, sources, columns)
    vmem = lambda shape, dtype: pltpu.VMEM(shape, dtype)
    scratch = [
        vmem((npt, nr, ntime), F32),
        vmem((npt, nr, ntime), F32),
        vmem((2, sources, columns), BF16),
        vmem((2, columns, sources), BF16),
        vmem((2, 2 * nf, ntime), BF16),
        vmem((2, 2 * nf, ntime), BF16),
        vmem((wide, ntime), F32),
        vmem((nf, 2, wide), BF16),
        vmem((nf, 2, wide), BF16),
        vmem((nx, nb, 2, wide), BF16),
        vmem((nx, nr // 4, 2 * nf, TILE), F32),
        vmem((2, columns, TILE), F32),
        vmem((2, sources, TILE), F32),
        vmem((nx, nr // 4, 2 * nf, TILE), F32),
        vmem((nx, 2 * nf, wide), I16),
        vmem((nx, 2 * nf, wide), I16),
        vmem((nf, 2, wide), I16),
        vmem((nf, 2, wide), I16),
        vmem((nf, 2, wide), BF16),
        vmem((nf, 2, wide), BF16),
        vmem((nx, nf, 2, wide), BF16),
        vmem((2, sources, TILE), F32),
        vmem((2, columns, TILE), F32),
        vmem((nx, nb, 2, wide), I16),
        vmem((nx, nb, 2, wide), I16),
        vmem((nf, 2, wide), I16),
        pltpu.SemaphoreType.DMA((5,)),
        pltpu.SemaphoreType.DMA((8,)),
        pltpu.SemaphoreType.DMA((8,)),
    ]
    hbm, inside = pl.BlockSpec(memory_space=pl.ANY), pl.BlockSpec(memory_space=pltpu.VMEM)
    out = jax.ShapeDtypeStruct((npt, nr, ntime), F32)
    return pl.pallas_call(
        functools.partial(kernel, (nf, nx, nr, npt)),
        out_shape=(out, out),
        in_specs=[hbm, hbm, inside, hbm, hbm, hbm],
        out_specs=(inside, inside),
        scratch_shapes=scratch,
        compiler_params=pltpu.CompilerParams(
            collective_id=0, has_side_effects=True, vmem_limit_bytes=48 * 1024 * 1024
        ),
        name="marchenko",
    )(direct, current, onsets, reflection, jnp.asarray(forward), jnp.asarray(inverse))


def solution(mesh):
    nf, nx = mesh.shape["freq"], mesh.shape["rows"]
    in_specs = (
        P("rows", "freq", None),
        P("rows", "freq", None),
        P("rows", "freq"),
        P(None, "freq", None, "rows"),
    )
    out_specs = (P("rows", "freq", None), P("rows", "freq", None))
    return jax.shard_map(
        functools.partial(shards, nf, nx), mesh=mesh, in_specs=in_specs, out_specs=out_specs, check_vma=False
    )
```

time: 234 us -> 106 us (0.45)
  blocking collectives: 115 us -> 0 us
  Pallas kernels: 0 us -> 96.8 us
  waiting for transfers between devices: 34.9 us -> 0 us
  local copies, waits for them, and re-layouts: 39.3 us -> 8.24 us
  starting transfers between devices: 17 us -> 0 us
  between operations: 14.4 us -> 0.66 us
  matrix products: 6.48 us -> 0 us
  other arithmetic: 5.79 us -> 0 us
    all_to_all x6 -> x0, blocking collectives: 104 us -> none  [the longest x2 53.1 us: to_freq(): lax.all_to_all(spectrum, 'freq', split_axis=1, concat_axis=3, tiled=True)]
    pallas_call x0 -> x1, Pallas kernels: none -> 96.8 us  [shards(): pl.pallas_call(functools.partial(kernel, (nf, nx, nr, npt)), out_shape=(o...]
    reduce_scatter x1 -> x0, waiting for transfers between devices: 20.6 us -> none  [shards(): lax.psum_scatter(partial_value, 'rows', scatter_dimension=3, tiled=True)]
    all_to_all x1 -> x0, starting transfers between devices: 17 us -> none  [to_time(): lax.all_to_all(spectrum, 'freq', split_axis=3, concat_axis=1, tiled=True)]
    unnamed x38 -> x9, local copies, waits for them, and re-layouts: 23.1 us -> 6.46 us
    all_to_all x1 -> x0, waiting for transfers between devices: 14.3 us -> none  [to_time(): lax.all_to_all(spectrum, 'freq', split_axis=3, concat_axis=1, tiled=True)]
    all_gather x1 -> x0, blocking collectives: 10.8 us -> none  [shards(): lax.all_gather(spec_up, 'rows', axis=2, tiled=True)]
    all_to_all x9 -> x0, local copies, waits for them, and re-layouts: 10.1 us -> none  [the longest x3 3.73 us: to_time(): lax.all_to_all(spectrum, 'freq', split_axis=3, concat_axis=1, tiled=True)]
  transfers between devices with their start and end apart: 2 -> 0, of which waited for: 2 -> 0; matrix products, arithmetic and copies ran while one was open for 1% -> 0% of each run, Pallas kernels for 0% -> 0%
where the time goes in v1:
time: 106 us
  Pallas kernels  96.8 us (91%)
  local copies, waits for them, and re-layouts  8.24 us (8%)
    pallas_call x1, Pallas kernels, shards(): pl.pallas_call(functools.partial(kernel, (nf, nx, nr, npt)), out_shape=(o...  96.8 us
    unnamed x9, local copies, waits for them, and re-layouts  6.46 us

profile of v1, /device:TPU:1, one launch (start us, length us, event | category | flops | bytes accessed | tf_op | source)
XLA Modules:
  0.0 105.7 jit_solution(1833023798072618704)
XLA Ops:
  0.6 0.8 copy.10.onsets_ref
  1.4 1.1 %copy.8.direct_hbm = f32[24,12,256]{2,1,0:T(8,128)S(1)} copy(f32[24,12,256]{2,0,1:T(8,128)} %param.6) | data formatting | bytes 589824 | tf_op args[0]
  2.5 1.1 %copy.9.current_hbm = f32[24,12,256]{2,1,0:T(8,128)S(1)} copy(f32[24,12,256]{2,0,1:T(8,128)} %param.7) | data formatting | bytes 589824 | tf_op args[1]
  3.5 0.0 copy-start
  3.5 1.7 %copy-done = bf16[2,1,1536,384]{3,2,1,0:T(8,128)(2,1)S(1)} copy-done((bf16[2,1,1536,384]{3,2,1,0:T(8,128)(2,1)S(1)}, bf16[2,1,1536,384]{3,2,1,0:T(8,128)(2,1)}, u32[]{:S(2)}) %copy-start) | copy-done | bytes 2359320
  5.2 0.0 copy-start.1
  5.2 0.9 copy-done.1
  6.2 0.0 copy-start.2
  6.2 0.9 copy-done.2
  7.1 96.8 %marchenko.1 = (f32[24,12,256]{2,1,0:T(8,128)S(1)}, f32[24,12,256]{2,1,0:T(8,128)S(1)}) custom-call(f32[24,12,256]{2,1,0:T(8,128)S(1)} %copy.8.direct_hbm, f32[24,12,256]{2,1,0:T(8,128)S(1)} %copy.9.current_hbm, s32[24,12]{1,0:T(8,128)S(1)} %copy.10.onsets_ref, bf16[2,1536,384]{2,1,0:T(8,128)(2,1)S(1)} %bitcast.1, bf16[2,256,256]{2,1,0:T(8,128)(2,1)S(1)} %copy-done.2, ...), custom_call_target="tpu_custom_call" | custom-call | tf_op jit(solution)/shard_map/marchenko/pallas_call | solution.py:310
  103.9 0.9 copy.11
  104.8 0.9 copy.12
Async XLA Ops:
  3.5 1.7 %copy-start = (bf16[2,1,1536,384]{3,2,1,0:T(8,128)(2,1)S(1)}, bf16[2,1,1536,384]{3,2,1,0:T(8,128)(2,1)}, u32[]{:S(2)}) copy-start(bf16[2,1,1536,384]{3,2,1,0:T(8,128)(2,1)} %param.9) | copy-start | bytes 7077892
  5.2 0.9 copy-start.1
  6.2 0.9 copy-start.2

commit v2 on v1

v2 whole, which is shorter than its diff:
```python
import functools
import math

import jax
import jax.numpy as jnp
import ml_dtypes
import numpy as np
from jax import lax
from jax.experimental import pallas as pl
from jax.experimental.pallas import tpu as pltpu
from jax.sharding import PartitionSpec as P

MESH = pl.DeviceIdType.MESH
PAD = 32
TILE = 128
PEAK = 32000.0
SPOT = 31
F32, BF16, I16 = jnp.float32, jnp.bfloat16, jnp.int16


def split(table):
    high = table.astype(ml_dtypes.bfloat16)
    low = (table - high.astype(np.float64)).astype(ml_dtypes.bfloat16)
    return np.stack([high, low])


def tables(nfreq, ntime):
    phase = (np.arange(nfreq)[:, None] * np.arange(ntime)[None, :] % ntime) * (2.0 * math.pi / ntime)
    weights = np.where(np.arange(nfreq) == 0, 1.0, 2.0)[:, None] / ntime
    forward = np.stack([np.cos(phase), -np.sin(phase)], axis=1)
    inverse = forward * weights[:, None]
    return (
        split(forward.reshape(2 * nfreq, ntime)),
        split(inverse.reshape(2 * nfreq, ntime)),
    )


def halves(value):
    high = value.astype(BF16)
    return high, (value - high.astype(F32)).astype(BF16)


def dot(a, b, contract):
    return lax.dot_general(a, b, (contract, ((), ())), preferred_element_type=F32)


def swap_blocks(arrays):
    shape = arrays[0].shape
    block = lax.broadcasted_iota(jnp.int32, shape, len(shape) - 1) // PAD
    low, even = block < 2, block % 2 == 0
    a0, a1, a2, a3 = arrays
    turn = lambda a, shift: pltpu.roll(a, shift, len(shape) - 1)
    b0, b2 = jnp.where(low, a0, turn(a2, 64)), jnp.where(low, turn(a0, 64), a2)
    b1, b3 = jnp.where(low, a1, turn(a3, 64)), jnp.where(low, turn(a1, 64), a3)
    c0, c1 = jnp.where(even, b0, turn(b1, 32)), jnp.where(even, turn(b0, 96), b1)
    c2, c3 = jnp.where(even, b2, turn(b3, 32)), jnp.where(even, turn(b2, 96), b3)
    return [c0, c1, c2, c3]


def encode(value):
    lane = lax.broadcasted_iota(jnp.int32, value.shape, 1)
    largest = jnp.max(jnp.abs(value), axis=1, keepdims=True)
    power = jnp.ceil(jnp.log2(jnp.maximum(largest, 1e-30)) + 1e-3)
    codes = jnp.round(value * (jnp.exp2(-power) * PEAK))
    return jnp.where(lane == SPOT, power, codes).astype(jnp.int32).astype(I16)


def decode(codes):
    codes = codes.astype(jnp.int32).astype(F32)
    return codes * (jnp.exp2(codes[:, SPOT : SPOT + 1]) * (1.0 / PEAK))


def kernel(
    dims,
    direct_hbm, current_hbm, onsets_ref, reflection_hbm, forward_hbm, inverse_hbm,
    up_ref, down_ref,
    direct_ref, current_ref, refl, back, forward_ref, inverse_ref, field, window,
    send_a, got_a, cols_a, stage, weights,
    partial, blocks, send_s, got_s, send_b, got_b,
    send_c, got_c, all_c, full, product,
    send_e, got_e, got_d,
    load_sem, send_sem, recv_sem, recv_a, recv_s, recv_c, recv_g, recv_e,
):
    nf, nx, nr, npt = dims
    nb = nf // nx
    rows = 2 * nf
    wide = nr * PAD
    ny = 2 * nx
    nzc = nf // ny
    f, x = lax.axis_index("freq"), lax.axis_index("rows")
    y, zc = f // nzc, lax.rem(f, nzc)

    loads = [
        pltpu.make_async_copy(source, target, load_sem.at[i])
        for i, (source, target) in enumerate(
            [
                (current_hbm, current_ref),
                (forward_hbm, forward_ref),
                (reflection_hbm, refl),
                (inverse_hbm, inverse_ref),
                (direct_hbm, direct_ref),
            ]
        )
    ]
    for load in loads:
        load.start()

    def offset(count, i):
        if isinstance(i, int):
            return count // 2 + (i + 1) // 2 * (1 - 2 * (i % 2))
        return count // 2 + lax.div(i + 1, 2) * (1 - 2 * lax.rem(i, 2))

    def group(i):
        return lax.rem(y + offset(ny, i), ny)

    def members(row, act, own):
        for j in range(nzc - (not own)):
            act(row * nzc + lax.rem(zc + offset(nzc, j), nzc))

    def each_group(act):
        def one(i, carry):
            act(i, group(i), True)
            return carry

        lax.fori_loop(0, ny - 1, one, 0)
        act(ny - 1, y, False)

    def each_group_near(act):
        act(ny - 1, y, False)

        def one(i, carry):
            act(ny - 1 - i, group(ny - 1 - i), True)
            return carry

        lax.fori_loop(1, ny, one, 0)

    def part(row, size=None):
        size = nzc if size is None else size
        return pl.ds(pl.multiple_of(row * size, size), size)

    barrier = pltpu.get_barrier_semaphore()

    def greet(peer):
        pl.semaphore_signal(barrier, inc=1, device_id=(peer, x), device_id_type=MESH)

    each_group(lambda i, row, own: members(row, greet, own))
    for step in range(1, nx):
        pl.semaphore_signal(barrier, inc=1, device_id=(f, lax.rem(x + step, nx)), device_id_type=MESH)

    def message(source, target, send, recv, peer):
        pltpu.make_async_remote_copy(
            src_ref=source, dst_ref=target, send_sem=send, recv_sem=recv, device_id=peer, device_id_type=MESH
        ).start()

    def deliver(source, target, which, recv, row, own):
        members(
            row,
            lambda peer: message(source.at[peer], target.at[f], send_sem.at[which], recv, (peer, x)),
            own,
        )

    def arrived(ref, count, sem):
        pltpu.make_async_copy(ref.at[pl.ds(0, count)], ref.at[pl.ds(0, count)], sem).wait()

    def transform():
        high, low = halves(field[...])
        spectra = (
            dot(forward_ref[0], high, ((1,), (1,)))
            + dot(forward_ref[0], low, ((1,), (1,)))
            + dot(forward_ref[1], high, ((1,), (1,)))
        )
        return spectra.astype(BF16).reshape(nf, 2, wide)

    def invert(messages):
        high, low = halves(decode(messages.reshape(rows, wide)))
        return (
            dot(high, inverse_ref[0], ((0,), (0,)))
            + dot(low, inverse_ref[0], ((0,), (0,)))
            + dot(high, inverse_ref[1], ((0,), (0,)))
        )

    def fill_window():
        samples = lax.broadcasted_iota(jnp.int32, (npt, 2 * nf), 1).astype(F32)
        own = lax.broadcasted_iota(jnp.int32, (npt, npt), 0) == lax.broadcasted_iota(jnp.int32, (npt, npt), 1)
        window[...] = jnp.zeros_like(window)
        for r in range(nr):
            spread_out = jnp.where(own, onsets_ref[r : r + 1, :].astype(F32), 0.0)
            start = jnp.sum(spread_out, axis=1, keepdims=True)
            inside = (samples < start) | (samples > 2 * nf - start)
            window[r * PAD : r * PAD + npt, :] = jnp.where(inside, 1.0, 0.0)

    def spread(messages, count, target, g):
        for i in range(nx):
            rows_in = messages(i).reshape(2 * count, wide).astype(F32)
            for t in range(nr // 4):
                stage[i, t, : 2 * count] = rows_in[:, t * TILE : (t + 1) * TILE]
        for t in range(nr // 4):
            for c in range(2):
                parts = swap_blocks([stage[i, t, pl.ds(c, count, stride=2), :] for i in range(nx)])
                for j in range(4):
                    target[c, g, pl.ds(4 * t + j, count, stride=nr), :] = parts[j]

    def gather(source, count, target):
        for t in range(nr // 4):
            for c in range(2):
                parts = swap_blocks([source[c, pl.ds(4 * t + j, count, stride=nr), :] for j in range(4)])
                for i in range(nx):
                    target[i, t, pl.ds(c, count, stride=2), :] = parts[i]

    def joined(source, i, where):
        return jnp.concatenate([source[i, t, where] for t in range(nr // 4)], axis=1)

    field[...] = jnp.zeros_like(field)
    loads[0].wait()
    for r in range(nr):
        field[r * PAD : r * PAD + npt, :] = current_ref[r]
    loads[1].wait()
    send_a[...] = transform()
    pl.semaphore_wait(barrier, nf - 1 + nx - 1)
    each_group(lambda i, row, own: deliver(send_a, got_a, 0, recv_a.at[y], row, own))
    got_a[f] = send_a[f]
    loads[2].wait()
    for c in range(2):
        back[c] = jnp.swapaxes(refl[c], 0, 1)
    fill_window()

    def to_columns(i, row, own):
        arrived(got_a, nzc if own else nzc - 1, recv_a.at[row])
        holder, half = lax.div(row, 2), lax.rem(row, 2)

        @pl.when(holder != x)
        def _():
            message(
                got_a.at[part(row)], cols_a.at[x, part(half)], send_sem.at[1], recv_sem.at[1], (f, holder)
            )

    each_group_near(to_columns)
    cols_a[x] = got_a[part(x, nb)]
    arrived(send_a, nf - 1, send_sem.at[0])
    arrived(send_a, nb * (nx - 1), send_sem.at[1])
    arrived(send_a, nb * (nx - 1), recv_sem.at[1])

    spread(lambda i: cols_a[i], nb, weights, 0)
    real, imag = weights[0, 0].astype(BF16), weights[1, 0].astype(BF16)
    sums = dot(refl[0], jnp.concatenate([real, imag], axis=1), ((1,), (0,))) + dot(
        refl[1], jnp.concatenate([-imag, real], axis=1), ((1,), (0,))
    )
    partial[0], partial[1] = sums[:, :TILE], sums[:, TILE:]
    gather(partial, nf, blocks)

    def scatter(i, row, own):
        where = part(row, 2 * nzc)
        for step in range(1, nx):
            peer = lax.rem(x + step, nx)
            send_s[peer, where] = encode(joined(blocks, peer, where))
            message(
                send_s.at[peer, where], got_s.at[x, where], send_sem.at[2], recv_s.at[i], (f, peer)
            )

    each_group(scatter)

    def collect(i, row, own):
        where = part(row, 2 * nzc)
        arrived(got_s.at[0], 2 * nzc * (nx - 1), recv_s.at[i])
        total = joined(blocks, x, where)
        for step in range(1, nx):
            total = total + decode(got_s[lax.rem(x + step, nx), where])
        send_b[part(row)] = encode(total).reshape(nzc, 2, wide)
        deliver(send_b, got_b, 3, recv_sem.at[3], row, own)

    each_group(collect)
    got_b[f] = send_b[f]
    loads[3].wait()
    for i in range(nx - 1):
        arrived(send_s.at[0], rows, send_sem.at[2])
    arrived(send_b, nf - 1, send_sem.at[3])
    arrived(got_b, nf - 1, recv_sem.at[3])

    field[...] = invert(got_b[...]) * window[...]
    for r in range(nr):
        up_ref[r] = field[r * PAD : r * PAD + npt, :]

    send_c[...] = transform()
    each_group_near(lambda i, row, own: deliver(send_c, got_c, 4, recv_c.at[y], row, own))
    got_c[f] = send_c[f]

    def to_all(i, row, own):
        arrived(got_c, nzc if own else nzc - 1, recv_c.at[row])
        for step in range(1, nx):
            peer = lax.rem(x + step, nx)
            message(
                got_c.at[part(row)], all_c.at[x, part(row)], send_sem.at[5], recv_g.at[i], (f, peer)
            )
        all_c[x, part(row)] = got_c[part(row)]

    each_group_near(to_all)

    def take(i, row, own):
        arrived(got_c, nzc * (nx - 1), recv_g.at[i])
        spread(lambda s: all_c[s, part(row)], nzc, full, row)

    each_group_near(take)
    arrived(send_c, nf - 1, send_sem.at[4])
    for i in range(nx - 1):
        arrived(got_c, nf, send_sem.at[5])

    real, imag = full[0].reshape(nf * nr, TILE).astype(BF16), full[1].reshape(nf * nr, TILE).astype(BF16)
    sums = dot(back[0], jnp.concatenate([real, imag], axis=1), ((1,), (0,))) + dot(
        back[1], jnp.concatenate([imag, -real], axis=1), ((1,), (0,))
    )
    product[0], product[1] = sums[:, :TILE], sums[:, TILE:]
    gather(product, nb, stage)

    for step in (2, 1, 3, 0):
        peer = lax.rem(x + step, nx)
        send_e[peer] = encode(joined(stage, peer, pl.ds(0, 2 * nb))).reshape(nb, 2, wide)
        if step:
            message(send_e.at[peer], got_e.at[x], send_sem.at[6], recv_e.at[x], (f, peer))
    got_e[x] = send_e[x]
    for step in (0, 1, 3, 2):
        origin = lax.rem(x + step, nx)
        if step:
            arrived(got_e.at[0], nb, recv_e.at[origin])
        for half in range(2):
            row = 2 * origin + half

            def pass_on(peer):
                place = got_e.at[origin, peer - origin * nb]
                message(place, got_d.at[f], send_sem.at[7], recv_sem.at[7], (peer, x))

            members(row, pass_on, False)

            @pl.when(row != y)
            def _():
                pass_on(row * nzc + zc)

    got_d[f] = got_e[f // nb, lax.rem(f, nb)]
    loads[4].wait()
    for i in range(nx - 1):
        arrived(got_e.at[0], nb, send_sem.at[6])
    arrived(got_d, nf - 1, send_sem.at[7])
    arrived(got_d, nf - 1, recv_sem.at[7])
    signal = invert(got_d[...]) * window[...]
    for r in range(nr):
        down_ref[r] = direct_ref[r] + signal[r * PAD : r * PAD + npt]


def shards(nf, nx, direct, current, onsets, reflection):
    npt, nr, ntime = current.shape
    nb, wide = nf // nx, nr * PAD
    sources, columns = nf * nr, nb * nr
    forward, inverse = tables(nf, ntime)
    reflection = reflection.reshape(2, sources, columns)
    vmem = lambda shape, dtype: pltpu.VMEM(shape, dtype)
    scratch = [
        vmem((nr, npt, ntime), F32),
        vmem((nr, npt, ntime), F32),
        vmem((2, sources, columns), BF16),
        vmem((2, columns, sources), BF16),
        vmem((2, 2 * nf, ntime), BF16),
        vmem((2, 2 * nf, ntime), BF16),
        vmem((wide, ntime), F32),
        vmem((wide, ntime), F32),
        vmem((nf, 2, wide), BF16),
        vmem((nf, 2, wide), BF16),
        vmem((nx, nb, 2, wide), BF16),
        vmem((nx, nr // 4, 2 * nf, TILE), F32),
        vmem((2, 1, columns, TILE), F32),
        vmem((2, sources, TILE), F32),
        vmem((nx, nr // 4, 2 * nf, TILE), F32),
        vmem((nx, 2 * nf, wide), I16),
        vmem((nx, 2 * nf, wide), I16),
        vmem((nf, 2, wide), I16),
        vmem((nf, 2, wide), I16),
        vmem((nf, 2, wide), BF16),
        vmem((nf, 2, wide), BF16),
        vmem((nx, nf, 2, wide), BF16),
        vmem((2, 2 * nx, sources // (2 * nx), TILE), F32),
        vmem((2, columns, TILE), F32),
        vmem((nx, nb, 2, wide), I16),
        vmem((nx, nb, 2, wide), I16),
        vmem((nf, 2, wide), I16),
        pltpu.SemaphoreType.DMA((5,)),
        pltpu.SemaphoreType.DMA((8,)),
        pltpu.SemaphoreType.DMA((8,)),
        pltpu.SemaphoreType.DMA((2 * nx,)),
        pltpu.SemaphoreType.DMA((2 * nx,)),
        pltpu.SemaphoreType.DMA((2 * nx,)),
        pltpu.SemaphoreType.DMA((2 * nx,)),
        pltpu.SemaphoreType.DMA((nx,)),
    ]
    by_receiver = lambda a: jnp.swapaxes(a, 0, 1)
    hbm, inside = pl.BlockSpec(memory_space=pltpu.HBM), pl.BlockSpec(memory_space=pltpu.VMEM)
    out = pltpu.VMEM((nr, npt, ntime), F32)
    up, down = pl.pallas_call(
        functools.partial(kernel, (nf, nx, nr, npt)),
        out_shape=(out, out),
        in_specs=[hbm, hbm, inside, hbm, hbm, hbm],
        out_specs=(inside, inside),
        scratch_shapes=scratch,
        compiler_params=pltpu.CompilerParams(
            collective_id=0, has_side_effects=True, vmem_limit_bytes=63 * 1024 * 1024
        ),
        name="marchenko",
    )(
        by_receiver(direct), by_receiver(current), by_receiver(onsets),
        reflection, jnp.asarray(forward), jnp.asarray(inverse),
    )
    return by_receiver(up), by_receiver(down)


def solution(mesh):
    nf, nx = mesh.shape["freq"], mesh.shape["rows"]
    in_specs = (
        P("rows", "freq", None),
        P("rows", "freq", None),
        P("rows", "freq"),
        P(None, "freq", None, "rows"),
    )
    out_specs = (P("rows", "freq", None), P("rows", "freq", None))
    return jax.shard_map(
        functools.partial(shards, nf, nx), mesh=mesh, in_specs=in_specs, out_specs=out_specs, check_vma=False
    )
```

time: 106 us -> 84.4 us (0.80)
  the two profiles are of different devices: /device:TPU:1 before, /device:TPU:23 now
where the time goes in v2:
time: 84.4 us; the launch traced here: 84.2 us
  Pallas kernels  82.1 us (97%)
  local copies, waits for them, and re-layouts  1.43 us (2%)
    pallas_call x1, Pallas kernels, shards(): pl.pallas_call(functools.partial(kernel, (nf, nx, nr, npt)), out_shape=(o...  82.1 us

profile of v2, /device:TPU:23, one launch (start us, length us, event | category | flops | bytes accessed | tf_op | source)
XLA Modules:
  0.0 84.2 jit_solution(15324640328216950107)
XLA Ops:
  0.6 82.1 %marchenko.1 = (f32[12,24,256]{2,1,0:T(8,128)S(1)}, f32[12,24,256]{2,1,0:T(8,128)S(1)}) custom-call(f32[12,24,256]{2,1,0:T(8,128)} %bitcast.9, f32[12,24,256]{2,1,0:T(8,128)} %bitcast.10, s32[12,24]{1,0:T(8,128)} %bitcast.11, bf16[2,1536,384]{2,1,0:T(8,128)(2,1)} %bitcast.8, bf16[2,256,256]{2,1,0:T(8,128)(2,1)} %constant.4.clone.forward_hbm, ...), custom_call_target="tpu_custom_call" | custom-call | tf_op jit(solution)/shard_map/marchenko/pallas_call | solution.py:395
  82.8 0.7 copy.10
  83.5 0.7 copy.11

commit v3 on v2

v3 whole, which is shorter than its diff:
```python
import functools
import math

import jax
import jax.numpy as jnp
import ml_dtypes
import numpy as np
from jax import lax
from jax.experimental import pallas as pl
from jax.experimental.pallas import tpu as pltpu
from jax.sharding import PartitionSpec as P

MESH = pl.DeviceIdType.MESH
PART = 8
TILE = 128
PEAK = 32000.0
SPOT = 127
F32, BF16, I16 = jnp.float32, jnp.bfloat16, jnp.int16


def split(table):
    high = table.astype(ml_dtypes.bfloat16)
    low = (table - high.astype(np.float64)).astype(ml_dtypes.bfloat16)
    return np.stack([high, low])


def tables(nfreq, ntime):
    phase = (np.arange(nfreq)[:, None] * np.arange(ntime)[None, :] % ntime) * (2.0 * math.pi / ntime)
    weights = np.where(np.arange(nfreq) == 0, 1.0, 2.0)[:, None] / ntime
    forward = np.stack([np.cos(phase), -np.sin(phase)], axis=1)
    inverse = forward * weights[:, None]
    return (
        split(forward.reshape(2 * nfreq, ntime)),
        split(inverse.reshape(2 * nfreq, ntime)),
    )


def halves(value):
    high = value.astype(BF16)
    return high, (value - high.astype(F32)).astype(BF16)


def dot(a, b, contract):
    return lax.dot_general(a, b, (contract, ((), ())), preferred_element_type=F32)


def lanes(shape):
    return lax.broadcasted_iota(jnp.int32, shape, len(shape) - 1)


def turn(value, shift):
    return pltpu.roll(value, shift, len(value.shape) - 1)


def swap_blocks(arrays):
    arrays = list(arrays)
    lane = lanes(arrays[0].shape)
    for bit in (4, 2, 1):
        shift = PART * bit
        clear = (lane & shift) == 0
        for i in range(8):
            if not i & bit:
                a, b = arrays[i], arrays[i + bit]
                arrays[i] = jnp.where(clear, a, turn(b, shift))
                arrays[i + bit] = jnp.where(clear, turn(a, TILE - shift), b)
    return arrays


def encode(value):
    largest = jnp.max(jnp.abs(value), axis=1, keepdims=True)
    power = jnp.ceil(jnp.log2(jnp.maximum(largest, 1e-30)) + 1e-3)
    codes = jnp.round(value * (jnp.exp2(-power) * PEAK))
    return jnp.where(lanes(value.shape) == SPOT, power, codes).astype(jnp.int32).astype(I16)


def decode(codes):
    codes = codes.astype(jnp.int32).astype(F32)
    return codes * (jnp.exp2(codes[:, SPOT : SPOT + 1]) * (1.0 / PEAK))


def kernel(
    dims,
    direct_hbm, current_hbm, onsets_ref, reflection_hbm, forward_hbm, inverse_hbm,
    up_ref, down_ref,
    direct_ref, current_ref, refl, back, forward_ref, inverse_ref, field, window,
    send_a, got_a, cols_a, stage, weights,
    partial, blocks, mine, send_s, got_s, send_b, got_b,
    send_c, got_c, all_c, full, product,
    send_e, got_e, got_d,
    load_sem, send_sem, recv_a, recv_q, recv_s, recv_b, recv_c, recv_g, recv_e, recv_d,
):
    nf, nx, nr, npt = dims
    nb = nf // nx
    rows = 2 * nf
    chunks = npt // PART
    ny = 2 * nx
    nzc = nf // ny
    f, x = lax.axis_index("freq"), lax.axis_index("rows")
    y, zc = f // nzc, lax.rem(f, nzc)

    loads = [
        pltpu.make_async_copy(source, target, load_sem.at[i])
        for i, (source, target) in enumerate(
            [
                (current_hbm, current_ref),
                (forward_hbm, forward_ref),
                (reflection_hbm, refl),
                (inverse_hbm, inverse_ref),
                (direct_hbm, direct_ref),
            ]
        )
    ]
    for load in loads:
        load.start()

    def offset(count, i):
        if isinstance(i, int):
            return count // 2 + (i + 1) // 2 * (1 - 2 * (i % 2))
        return count // 2 + lax.div(i + 1, 2) * (1 - 2 * lax.rem(i, 2))

    def group(i):
        return lax.rem(y + offset(ny, i), ny)

    def members(row, act, own):
        for j in range(nzc - (not own)):
            act(row * nzc + lax.rem(zc + offset(nzc, j), nzc))

    def every(row, act):
        members(row, act, False)

        @pl.when(row != y)
        def _():
            act(row * nzc + zc)

    def each_group(act):
        def one(i, carry):
            act(i, group(i), True)
            return carry

        lax.fori_loop(0, ny - 1, one, 0)
        act(ny - 1, y, False)

    def each_group_near(act):
        act(ny - 1, y, False)

        def one(i, carry):
            act(ny - 1 - i, group(ny - 1 - i), True)
            return carry

        lax.fori_loop(1, ny, one, 0)

    def part(row, size=None):
        size = nzc if size is None else size
        return pl.ds(pl.multiple_of(row * size, size), size)

    barrier = pltpu.get_barrier_semaphore()

    def greet(peer):
        pl.semaphore_signal(barrier, inc=1, device_id=(peer, x), device_id_type=MESH)

    each_group(lambda i, row, own: members(row, greet, own))
    for step in range(1, nx):
        pl.semaphore_signal(barrier, inc=1, device_id=(f, lax.rem(x + step, nx)), device_id_type=MESH)

    def message(source, target, send, recv, peer):
        pltpu.make_async_remote_copy(
            src_ref=source, dst_ref=target, send_sem=send, recv_sem=recv, device_id=peer, device_id_type=MESH
        ).start()

    def deliver(source, target, send, recv, row, own):
        members(
            row,
            lambda peer: message(source.at[peer], target.at[f], send, recv, (peer, x)),
            own,
        )

    def arrived(ref, count, sem):
        pltpu.make_async_copy(ref.at[pl.ds(0, count)], ref.at[pl.ds(0, count)], sem).wait()

    def transform(ch):
        high, low = halves(field[ch])
        spectra = (
            dot(forward_ref[0], high, ((1,), (1,)))
            + dot(forward_ref[0], low, ((1,), (1,)))
            + dot(forward_ref[1], high, ((1,), (1,)))
        )
        return spectra.astype(BF16).reshape(nf, 2, TILE)

    def invert(messages):
        high, low = halves(decode(messages.reshape(rows, TILE)))
        return (
            dot(high, inverse_ref[0], ((0,), (0,)))
            + dot(low, inverse_ref[0], ((0,), (0,)))
            + dot(high, inverse_ref[1], ((0,), (0,)))
        )

    def fill_window():
        samples = lax.broadcasted_iota(jnp.int32, (npt, 2 * nf), 1).astype(F32)
        own = lax.broadcasted_iota(jnp.int32, (npt, npt), 0) == lax.broadcasted_iota(jnp.int32, (npt, npt), 1)
        window[...] = jnp.zeros_like(window)
        for r in range(nr):
            spread_out = jnp.where(own, onsets_ref[r : r + 1, :].astype(F32), 0.0)
            start = jnp.sum(spread_out, axis=1, keepdims=True)
            inside = (samples < start) | (samples > 2 * nf - start)
            kept = jnp.where(inside, 1.0, 0.0)
            for ch in range(chunks):
                window[ch, r * PART : (r + 1) * PART, :] = kept[ch * PART : (ch + 1) * PART]

    def each_chunk(act):
        def one(ch, carry):
            act(ch)
            return carry

        lax.fori_loop(0, chunks, one, 0)

    def points(ch):
        return pl.ds(pl.multiple_of(ch * PART, PART), PART)

    def spread(messages, count, target):
        for i in range(nx):
            stage[i, : 2 * count] = messages(i).reshape(2 * count, TILE).astype(F32)
        step = min(count, 32)
        for q in range(0, count, step):
            parts = swap_blocks(
                [stage[i, pl.ds(2 * q + c, step, stride=2), :] for c in range(2) for i in range(nx)]
            )
            for r in range(nr):
                part = parts[r] if r < 8 else turn(parts[r - 8], TILE // 2)
                target[pl.ds(q * nr + r, step, stride=nr), :] = part

    def gather(source, count, target):
        step = min(count, 32)
        for q in range(0, count, step):
            low = lanes((step, TILE)) < TILE // 2
            parts = [source[pl.ds(q * nr + r, step, stride=nr), :] for r in range(nr)]
            above = [turn(part, TILE // 2) for part in parts[8:]]
            above += [jnp.zeros((step, TILE), F32)] * (8 - len(above))
            parts = swap_blocks([jnp.where(low, a, b) for a, b in zip(parts[:8], above)])
            for c in range(2):
                for i in range(nx):
                    target[i, pl.ds(2 * q + c, step, stride=2), :] = parts[c * nx + i]

    def crossed(value, sign):
        low = lanes(value.shape) < TILE // 4
        return jnp.where(low, -sign * turn(value, TILE - TILE // 4), sign * turn(value, TILE // 4)).astype(BF16)

    field[...] = jnp.zeros_like(field)
    loads[0].wait()
    for r in range(nr):
        for ch in range(chunks):
            field[ch, r * PART : (r + 1) * PART, :] = current_ref[r, ch * PART : (ch + 1) * PART, :]
    loads[1].wait()

    def start_a(ch):
        send_a[ch] = transform(ch)

    each_chunk(start_a)
    pl.semaphore_wait(barrier, nf - 1 + nx - 1)

    def first(ch):
        each_group(
            lambda i, row, own: deliver(
                send_a.at[ch], got_a.at[ch], send_sem.at[0, ch], recv_a.at[ch, y], row, own
            )
        )
        got_a[ch, f] = send_a[ch, f]

    each_chunk(first)
    loads[2].wait()
    for c in range(2):
        back[c] = jnp.swapaxes(refl[c], 0, 1)
    fill_window()

    def columns(ch):
        def forward(i, row, own):
            arrived(got_a.at[ch], nzc if own else nzc - 1, recv_a.at[ch, row])
            holder, half = lax.div(row, 2), lax.rem(row, 2)

            @pl.when(holder != x)
            def _():
                message(
                    got_a.at[ch, part(row)], cols_a.at[ch, x, part(half)],
                    send_sem.at[1, ch], recv_q.at[ch], (f, holder),
                )

        each_group_near(forward)
        cols_a[ch, x] = got_a[ch, part(x, nb)]

    each_chunk(columns)

    def products(ch):
        arrived(got_a.at[0], nb * (nx - 1), recv_q.at[ch])
        spread(lambda i: cols_a[ch, i], nb, weights)
        value = weights[...]
        partial[...] = dot(refl[0], value.astype(BF16), ((1,), (0,))) + dot(
            refl[1], crossed(value, 1.0), ((1,), (0,))
        )
        gather(partial, nf, blocks)
        mine[ch] = blocks[x]
        for step in range(1, nx):
            peer = lax.rem(x + step, nx)
            send_s[ch, peer] = encode(blocks[peer])
        for away in (2, 1, 3, 0):
            place = lax.rem(f // nb + away, nx)
            where = part(place, 2 * nb)
            for step in (2, 1, 3):
                peer = lax.rem(x + step, nx)
                message(
                    send_s.at[ch, peer, where], got_s.at[ch, x, where],
                    send_sem.at[2, ch], recv_s.at[ch, away], (f, peer),
                )

    each_chunk(products)

    def collect(ch):
        for away in (2, 1, 3, 0):
            place = lax.rem(f // nb + away, nx)
            where = part(place, 2 * nb)
            arrived(got_s.at[0, 0], 2 * nb * (nx - 1), recv_s.at[ch, away])
            total = mine[ch, where]
            for step in range(1, nx):
                total = total + decode(got_s[ch, lax.rem(x + step, nx), where])
            send_b[ch, part(place, nb)] = encode(total).reshape(nb, 2, TILE)
            for half in range(2):
                every(
                    2 * place + half,
                    lambda peer: message(
                        send_b.at[ch, peer], got_b.at[ch, f], send_sem.at[3, ch], recv_b.at[ch], (peer, x)
                    ),
                )
        got_b[ch, f] = send_b[ch, f]

    each_chunk(collect)
    loads[3].wait()

    def upward(ch):
        arrived(got_b.at[ch], nf - 1, recv_b.at[ch])
        field[ch] = invert(got_b[ch]) * window[ch]
        send_c[ch] = transform(ch)
        each_group_near(
            lambda i, row, own: deliver(
                send_c.at[ch], got_c.at[ch], send_sem.at[4, ch], recv_c.at[ch, y], row, own
            )
        )
        got_c[ch, f] = send_c[ch, f]
        for r in range(nr):
            up_ref[r, points(ch), :] = field[ch, r * PART : (r + 1) * PART, :]

    each_chunk(upward)

    def to_all(ch):
        def forward(i, row, own):
            arrived(got_c.at[ch], nzc if own else nzc - 1, recv_c.at[ch, row])
            for step in (2, 1, 3):
                peer = lax.rem(x + step, nx)
                message(
                    got_c.at[ch, part(row)], all_c.at[ch, x, part(row)],
                    send_sem.at[5, ch], recv_g.at[ch], (f, peer),
                )

        each_group_near(forward)
        all_c[ch, x] = got_c[ch]

    each_chunk(to_all)

    def conjugate(ch):
        arrived(all_c.at[ch], nx - 1, recv_g.at[ch])
        spread(lambda i: all_c[ch, i], nf, full)
        value = full[...]
        product[...] = dot(back[0], value.astype(BF16), ((1,), (0,))) + dot(
            back[1], crossed(value, -1.0), ((1,), (0,))
        )
        gather(product, nb, stage)
        for step in (2, 1, 3, 0):
            peer = lax.rem(x + step, nx)
            send_e[ch, peer] = encode(stage[peer, : 2 * nb]).reshape(nb, 2, TILE)
            if step:
                message(send_e.at[ch, peer], got_e.at[ch, x], send_sem.at[6, ch], recv_e.at[ch, x], (f, peer))
        got_e[ch, x] = send_e[ch, x]

    def pass_on(ch, step):
        origin = lax.rem(x + step, nx)
        if step:
            arrived(got_e.at[0, 0], nb, recv_e.at[ch, origin])
        for half in range(2):
            every(
                2 * origin + half,
                lambda peer: message(
                    got_e.at[ch, origin, peer - origin * nb], got_d.at[ch, f],
                    send_sem.at[7, ch], recv_d.at[ch], (peer, x),
                ),
            )

    def others(ch):
        for step in (1, 3, 2):
            pass_on(ch, step)
        got_d[ch, f] = got_e[ch, f // nb, lax.rem(f, nb)]

    def backward(ch, carry):
        conjugate(ch)
        pass_on(ch, 0)

        @pl.when(ch > 0)
        def _():
            others(ch - 1)

        return carry

    lax.fori_loop(0, chunks, backward, 0)
    others(chunks - 1)
    loads[4].wait()

    def downward(ch):
        arrived(got_d.at[ch], nf - 1, recv_d.at[ch])
        signal = invert(got_d[ch]) * window[ch]
        for r in range(nr):
            down_ref[r, points(ch), :] = (
                direct_ref[r, points(ch), :] + signal[r * PART : (r + 1) * PART]
            )

    each_chunk(downward)

    def left(ch):
        for which, ref in ((0, send_a), (3, send_b), (4, send_c), (7, got_d)):
            arrived(ref.at[ch], nf - 1, send_sem.at[which, ch])
        for which in (1, 6):
            arrived(got_a.at[ch], nb * (nx - 1), send_sem.at[which, ch])
        arrived(send_s.at[ch], nx - 1, send_sem.at[2, ch])
        arrived(all_c.at[ch], nx - 1, send_sem.at[5, ch])

    each_chunk(left)


def shards(nf, nx, direct, current, onsets, reflection):
    npt, nr, ntime = current.shape
    nb, chunks = nf // nx, npt // PART
    sources, columns = nf * nr, nb * nr
    forward, inverse = tables(nf, ntime)
    reflection = reflection.reshape(2, sources, columns)
    vmem = lambda shape, dtype: pltpu.VMEM(shape, dtype)
    scratch = [
        vmem((nr, npt, ntime), F32),
        vmem((nr, npt, ntime), F32),
        vmem((2, sources, columns), BF16),
        vmem((2, columns, sources), BF16),
        vmem((2, 2 * nf, ntime), BF16),
        vmem((2, 2 * nf, ntime), BF16),
        vmem((chunks, TILE, ntime), F32),
        vmem((chunks, TILE, ntime), F32),
        vmem((chunks, nf, 2, TILE), BF16),
        vmem((chunks, nf, 2, TILE), BF16),
        vmem((chunks, nx, nb, 2, TILE), BF16),
        vmem((nx, 2 * nf, TILE), F32),
        vmem((columns, TILE), F32),
        vmem((sources, TILE), F32),
        vmem((nx, 2 * nf, TILE), F32),
        vmem((chunks, 2 * nf, TILE), F32),
        vmem((chunks, nx, 2 * nf, TILE), I16),
        vmem((chunks, nx, 2 * nf, TILE), I16),
        vmem((chunks, nf, 2, TILE), I16),
        vmem((chunks, nf, 2, TILE), I16),
        vmem((chunks, nf, 2, TILE), BF16),
        vmem((chunks, nf, 2, TILE), BF16),
        vmem((chunks, nx, nf, 2, TILE), BF16),
        vmem((sources, TILE), F32),
        vmem((columns, TILE), F32),
        vmem((chunks, nx, nb, 2, TILE), I16),
        vmem((chunks, nx, nb, 2, TILE), I16),
        vmem((chunks, nf, 2, TILE), I16),
        pltpu.SemaphoreType.DMA((5,)),
        pltpu.SemaphoreType.DMA((8, chunks)),
        pltpu.SemaphoreType.DMA((chunks, 2 * nx)),
        pltpu.SemaphoreType.DMA((chunks,)),
        pltpu.SemaphoreType.DMA((chunks, nx)),
        pltpu.SemaphoreType.DMA((chunks,)),
        pltpu.SemaphoreType.DMA((chunks, 2 * nx)),
        pltpu.SemaphoreType.DMA((chunks,)),
        pltpu.SemaphoreType.DMA((chunks, nx)),
        pltpu.SemaphoreType.DMA((chunks,)),
    ]
    by_receiver = lambda a: jnp.swapaxes(a, 0, 1)
    hbm, inside = pl.BlockSpec(memory_space=pltpu.HBM), pl.BlockSpec(memory_space=pltpu.VMEM)
    out = pltpu.VMEM((nr, npt, ntime), F32)
    up, down = pl.pallas_call(
        functools.partial(kernel, (nf, nx, nr, npt)),
        out_shape=(out, out),
        in_specs=[hbm, hbm, inside, hbm, hbm, hbm],
        out_specs=(inside, inside),
        scratch_shapes=scratch,
        compiler_params=pltpu.CompilerParams(
            collective_id=0, has_side_effects=True, vmem_limit_bytes=63 * 1024 * 1024
        ),
        name="marchenko",
    )(
        by_receiver(direct), by_receiver(current), by_receiver(onsets),
        reflection, jnp.asarray(forward), jnp.asarray(inverse),
    )
    return by_receiver(up), by_receiver(down)


def solution(mesh):
    nf, nx = mesh.shape["freq"], mesh.shape["rows"]
    in_specs = (
        P("rows", "freq", None),
        P("rows", "freq", None),
        P("rows", "freq"),
        P(None, "freq", None, "rows"),
    )
    out_specs = (P("rows", "freq", None), P("rows", "freq", None))
    return jax.shard_map(
        functools.partial(shards, nf, nx), mesh=mesh, in_specs=in_specs, out_specs=out_specs, check_vma=False
    )
```

time: 84.4 us -> 75.5 us (0.89)
  the two profiles are of different devices: /device:TPU:23 before, /device:TPU:1 now
where the time goes in v3:
time: 75.5 us; the launch traced here: 74.1 us
  Pallas kernels  72.1 us (95%)
  local copies, waits for them, and re-layouts  1.43 us (2%)
    pallas_call x1, Pallas kernels, shards(): pl.pallas_call(functools.partial(kernel, (nf, nx, nr, npt)), out_shape=(o...  72.1 us

profile of v3, /device:TPU:1, one launch (start us, length us, event | category | flops | bytes accessed | tf_op | source)
XLA Modules:
  0.0 74.1 jit_solution(3453603797101961453)
XLA Ops:
  0.6 72.1 %marchenko.1 = (f32[12,24,256]{2,1,0:T(8,128)S(1)}, f32[12,24,256]{2,1,0:T(8,128)S(1)}) custom-call(f32[12,24,256]{2,1,0:T(8,128)} %bitcast.9, f32[12,24,256]{2,1,0:T(8,128)} %bitcast.10, s32[12,24]{1,0:T(8,128)} %bitcast.11, bf16[2,1536,384]{2,1,0:T(8,128)(2,1)} %bitcast.8, bf16[2,256,256]{2,1,0:T(8,128)(2,1)} %constant.4.clone.forward_hbm, ...), custom_call_target="tpu_custom_call" | custom-call | tf_op jit(solution)/shard_map/marchenko/pallas_call | solution.py:484
  72.7 0.7 copy.10
  73.4 0.7 copy.11

commit v4 on v3

--- a/solution.py
+++ b/solution.py
@@ -337,7 +337,7 @@
         arrived(got_b.at[ch], nf - 1, recv_b.at[ch])
         field[ch] = invert(got_b[ch]) * window[ch]
         send_c[ch] = transform(ch)
-        each_group_near(
+        each_group(
             lambda i, row, own: deliver(
                 send_c.at[ch], got_c.at[ch], send_sem.at[4, ch], recv_c.at[ch, y], row, own
             )

time: 75.5 us -> 74.9 us (level)
  no operation moved by 1% of the time
where the time goes in v4:
time: 74.9 us; the launch traced here: 73.5 us
  Pallas kernels  71.4 us (95%)
  local copies, waits for them, and re-layouts  1.43 us (2%)
    pallas_call x1, Pallas kernels, shards(): pl.pallas_call(functools.partial(kernel, (nf, nx, nr, npt)), out_shape=(o...  71.4 us

profile of v4, /device:TPU:1, one launch (start us, length us, event | category | flops | bytes accessed | tf_op | source)
XLA Modules:
  0.0 73.5 jit_solution(635157322692623502)
XLA Ops:
  0.6 71.4 %marchenko.1 = (f32[12,24,256]{2,1,0:T(8,128)S(1)}, f32[12,24,256]{2,1,0:T(8,128)S(1)}) custom-call(f32[12,24,256]{2,1,0:T(8,128)} %bitcast.9, f32[12,24,256]{2,1,0:T(8,128)} %bitcast.10, s32[12,24]{1,0:T(8,128)} %bitcast.11, bf16[2,1536,384]{2,1,0:T(8,128)(2,1)} %bitcast.8, bf16[2,256,256]{2,1,0:T(8,128)(2,1)} %constant.4.clone.forward_hbm, ...), custom_call_target="tpu_custom_call" | custom-call | tf_op jit(solution)/shard_map/marchenko/pallas_call | solution.py:484
  72.1 0.7 copy.10
  72.8 0.7 copy.11
